TPU v7x, 32 devices: a whole 2x2x4 slice. The times are simulated.
32 devices in a mesh: dp: 8 (over z, core), mp: 4 (over y, x).
Axes of the slice: x: 2, y: 2, z: 4, core: 2. Of those that a mesh axis runs over, the one named last changes fastest.
Arguments:
- tokens: bfloat16 [6144, 2048], P('dp'), may hold values from -20 to 20
- cotangent: bfloat16 [6144, 2048], P('dp'), may hold values from -6 to 6
- w_gate: bfloat16 [2048, 8192], P(None, 'mp'), may hold values from -1 to 1
- w_up: bfloat16 [2048, 8192], P(None, 'mp'), may hold values from -1 to 1
- w_down: bfloat16 [8192, 2048], P('mp'), may hold values from -0.0625 to 0.0625
- row_gate: float32 [2048], P('dp'), may hold values from 0.0003 to 20
- col_gate: float32 [8192], P('mp'), may hold values from 0.0003 to 10
- row_up: float32 [2048], P('dp'), may hold values from 0.0003 to 20
- col_up: float32 [8192], P('mp'), may hold values from 0.0003 to 10
- row_down: float32 [8192], P(('mp', 'dp')), may hold values from 0.01 to 300
- col_down: float32 [2048], replicated, may hold values from 0.01 to 300
Outputs:
- token_grad: bfloat16 [6144, 2048], P('dp', 'mp')
- update_gate: float32 [2048, 8192], P('dp', 'mp')
- update_up: float32 [2048, 8192], P('dp', 'mp')
- update_down: float32 [8192, 2048], P(('mp', 'dp'))
- row_gate_new: float32 [2048], P('dp')
- col_gate_new: float32 [8192], P('mp')
- row_up_new: float32 [2048], P('dp')
- col_up_new: float32 [8192], P('mp')
- row_down_new: float32 [8192], P(('mp', 'dp'))
- col_down_new: float32 [2048], replicated
All inputs are finite; a program needn't handle non-finite values.
Results may differ from a plain program's by a relative error of at most 0.015.
Values may be sent and summed in bfloat16 or wider, within the bound.
A program may use at most 128 MiB of HBM per device.

v0:
```python
import jax
import jax.numpy as jnp
from jax import lax
from jax.sharding import PartitionSpec as P

epsilon_one = 1e-30
decay_rate = 0.8


def silu_parts(gate_pre):
    sig = jax.nn.sigmoid(gate_pre)
    return (gate_pre * sig, sig * (1.0 + gate_pre * (1.0 - sig)))


def moment_step(old_value, column_total, count):
    return decay_rate * old_value + (1.0 - decay_rate) * (column_total / count + epsilon_one)


def body(
    tokens, cotangent, w_gate, w_up, w_down, row_gate, col_gate, row_up, col_up, row_down, col_down
):
    data_count = lax.axis_size("dp")
    model_count = lax.axis_size("mp")
    tok_rows, width_model = tokens.shape
    units = w_gate.shape[1]
    all_units = units * model_count
    grad_scale = float(tok_rows * data_count) ** (-0.5)
    gate_pre = jnp.dot(tokens, w_gate, preferred_element_type=jnp.float32)
    up_pre = jnp.dot(tokens, w_up, preferred_element_type=jnp.float32)
    activated, derivative = silu_parts(gate_pre)
    hidden = (activated * up_pre).astype(jnp.bfloat16)
    hidden_grad = jnp.einsum("td,fd->tf", cotangent, w_down, preferred_element_type=jnp.float32)
    grad_gate = (hidden_grad * up_pre * derivative).astype(jnp.bfloat16)
    grad_up = (hidden_grad * activated).astype(jnp.bfloat16)

    def weight_term(left_side, right_side):
        return (
            jnp.einsum("tr,tc->rc", left_side, right_side, preferred_element_type=jnp.float32)
            * grad_scale
        )

    g_gate, g_up, g_down = (
        lax.psum_scatter(
            weight_term(tokens, grad_gate).astype(jnp.bfloat16),
            "dp",
            scatter_dimension=0,
            tiled=True,
        ).astype(jnp.float32),
        lax.psum_scatter(
            weight_term(tokens, grad_up).astype(jnp.bfloat16), "dp", scatter_dimension=0, tiled=True
        ).astype(jnp.float32),
        lax.psum_scatter(
            weight_term(hidden, cotangent).astype(jnp.bfloat16),
            "dp",
            scatter_dimension=0,
            tiled=True,
        ).astype(jnp.float32),
    )
    input_terms = jnp.einsum("tf,df->td", grad_gate, w_gate, preferred_element_type=jnp.float32)
    input_terms = input_terms + jnp.einsum(
        "tf,df->td", grad_up, w_up, preferred_element_type=jnp.float32
    )
    token_grad = lax.psum_scatter(
        input_terms.astype(jnp.bfloat16), "mp", scatter_dimension=1, tiled=True
    )
    squares_gate = g_gate * g_gate
    squares_up = g_up * g_up
    squares_down = g_down * g_down
    row_totals = lax.psum((jnp.sum(squares_gate, 1), jnp.sum(squares_up, 1)), "mp")
    col_totals = lax.psum((jnp.sum(squares_gate, 0), jnp.sum(squares_up, 0)), "dp")
    row_gate_new = moment_step(row_gate, row_totals[0], all_units)
    row_up_new = moment_step(row_up, row_totals[1], all_units)
    col_gate_new = moment_step(col_gate, col_totals[0], width_model)
    col_up_new = moment_step(col_up, col_totals[1], width_model)
    row_down_new = moment_step(row_down, jnp.sum(squares_down, 1), width_model)
    row_counts = jnp.array([width_model, width_model, all_units], jnp.float32)
    down_total = lax.psum(jnp.sum(squares_down, 0), ("dp", "mp"))
    new_sums = jnp.stack(
        [
            jnp.sum(row_gate_new) / model_count,
            jnp.sum(row_up_new) / model_count,
            jnp.sum(row_down_new),
        ]
    )
    row_means = lax.psum(new_sums, ("dp", "mp")) / row_counts
    col_down_new = moment_step(col_down, down_total, all_units)
    raw_gate = g_gate / jnp.sqrt(row_gate_new[:, None] * col_gate_new[None, :] / row_means[0])
    raw_up = g_up / jnp.sqrt(row_up_new[:, None] * col_up_new[None, :] / row_means[1])
    raw_down = g_down / jnp.sqrt(row_down_new[:, None] * col_down_new[None, :] / row_means[2])
    raw_totals = lax.psum(
        jnp.stack(
            [jnp.sum(raw_gate * raw_gate), jnp.sum(raw_up * raw_up), jnp.sum(raw_down * raw_down)]
        ),
        ("dp", "mp"),
    )
    divisor = jnp.maximum(1.0, jnp.sqrt(raw_totals / float(width_model * all_units)))
    update_gate = raw_gate / divisor[0]
    update_up = raw_up / divisor[1]
    update_down = raw_down / divisor[2]
    return (
        token_grad,
        update_gate,
        update_up,
        update_down,
        row_gate_new,
        col_gate_new,
        row_up_new,
        col_up_new,
        row_down_new,
        col_down_new,
    )


def solution(mesh):
    in_specs = (
        P("dp", None),
        P("dp", None),
        P(None, "mp"),
        P(None, "mp"),
        P("mp", None),
        P("dp"),
        P("mp"),
        P("dp"),
        P("mp"),
        P(("mp", "dp")),
        P(),
    )
    out_specs = (
        P("dp", "mp"),
        P("dp", "mp"),
        P("dp", "mp"),
        P(("mp", "dp"), None),
        P("dp"),
        P("mp"),
        P("dp"),
        P("mp"),
        P(("mp", "dp")),
        P(),
    )
    return jax.shard_map(body, mesh=mesh, in_specs=in_specs, out_specs=out_specs, check_vma=False)
```

profile of v0, /device:TPU:10, one launch (start us, length us, event | category | flops | bytes accessed | tf_op | source)
XLA Modules:
  0.0 467.0 jit_solution(7626841583861972148)
XLA Ops:
  7.2 1.8 copy-done
  9.1 10.8 %fusion.17 = f32[768,2048]{1,0:T(8,128)} fusion(bf16[768,2048]{1,0:T(8,128)(2,1)S(1)} %copy-done, bf16[2048,2048]{1,0:T(8,128)(2,1)} %param.14), kind=kOutput, calls=%fused_computation.45 | convolution fusion | flops 6442450944 | bytes 17825792 | tf_op jit(solution)/shard_map/dot_general | solution.py:28
  19.9 8.7 %fusion.16 = f32[768,2048]{1,0:T(8,128)} fusion(bf16[768,2048]{1,0:T(8,128)(2,1)S(1)} %copy-done, bf16[2048,2048]{1,0:T(8,128)(2,1)S(1)} %copy-done.16), kind=kOutput, calls=%fused_computation.44 | convolution fusion | flops 6442450944 | bytes 17825792 | tf_op jit(solution)/shard_map/dot_general | solution.py:29
  28.6 15.5 %multiply_convert_fusion.4 = (bf16[768,2048]{1,0:T(8,128)(2,1)}, bf16[768,2048]{1,0:T(8,128)(2,1)}) fusion(f32[768,2048]{1,0:T(8,128)} %fusion.17, f32[768,2048]{1,0:T(8,128)} %fusion.16, bf16[768,2048]{1,0:T(8,128)(2,1)S(1)} %copy-done.17, bf16[2048,2048]{1,0:T(8,128)(2,1)} %param.16), kind=kOutput, calls=%fused_computation.7 | convolution fusion | flops 6462898176 | bytes 30408704 | tf_op jit(solution)/shard_map/td,fd->tf/dot_general | solution.py:32
  44.0 10.9 %fusion.1 = bf16[2048,2048]{0,1:T(8,128)(2,1)} fusion(bf16[768,2048]{1,0:T(8,128)(2,1)} %get-tuple-element.38, bf16[768,2048]{1,0:T(8,128)(2,1)S(1)} %copy-done), kind=kOutput, calls=%fused_computation.4 | convolution fusion | flops 6450839552 | bytes 14680064 | tf_op jit(solution)/shard_map/tr,tc->rc/dot_general | solution.py:38
  55.1 10.9 %fusion = bf16[2048,2048]{0,1:T(8,128)(2,1)} fusion(bf16[768,2048]{1,0:T(8,128)(2,1)} %get-tuple-element.39, bf16[768,2048]{1,0:T(8,128)(2,1)S(1)} %copy-done), kind=kOutput, calls=%fused_computation.3 | convolution fusion | flops 6450839552 | bytes 14680064 | tf_op jit(solution)/shard_map/tr,tc->rc/dot_general | solution.py:38
  66.0 1.9 copy-done.18
  67.9 14.7 %multiply_convert_fusion = bf16[2048,2048]{1,0:T(8,128)(2,1)} fusion(bf16[768,2048]{1,0:T(8,128)(2,1)S(1)} %copy-done.18, f32[768,2048]{1,0:T(8,128)} %fusion.16, f32[768,2048]{1,0:T(8,128)} %fusion.17), kind=kOutput, calls=%fused_computation | convolution fusion | flops 6460276736 | bytes 24117248 | tf_op jit(solution)/shard_map/tr,tc->rc/dot_general | solution.py:38
  82.7 10.5 %fusion.18 = f32[768,2048]{1,0:T(8,128)S(1)} fusion(bf16[768,2048]{1,0:T(8,128)(2,1)} %get-tuple-element.39, bf16[2048,2048]{1,0:T(8,128)(2,1)} %param.14), kind=kOutput, calls=%fused_computation.46 | convolution fusion | flops 6442450944 | bytes 17825792 | tf_op jit(solution)/shard_map/tf,df->td/dot_general | solution.py:59
  93.3 10.3 %add_convert_fusion = bf16[768,2048]{1,0:T(8,128)(2,1)} fusion(f32[768,2048]{1,0:T(8,128)S(1)} %fusion.18, bf16[768,2048]{1,0:T(8,128)(2,1)S(1)} %copy-done.20, bf16[2048,2048]{1,0:T(8,128)(2,1)} %param.15), kind=kOutput, calls=%fused_computation.6 | convolution fusion | flops 6445596672 | bytes 20971520 | tf_op jit(solution)/shard_map/tf,df->td/dot_general | solution.py:60
  103.7 39.5 %reduce-scatter.9.cloned.1.call-done = bf16[256,2048]{0,1:T(8,128)(2,1)} async-done(((bf16[2048,2048]{0,1:T(8,128)(2,1)}), bf16[256,2048]{0,1:T(8,128)(2,1)}) %reduce-scatter.9.cloned.1.call-update) | async-done | bytes 1048592 | tf_op jit(solution)/shard_map/reduce_scatter | solution.py:49
  143.1 1.7 fusion.5
  144.8 88.6 %reduce-scatter.7.cloned.1.call-done = bf16[256,2048]{0,1:T(8,128)(2,1)} async-done(((bf16[2048,2048]{0,1:T(8,128)(2,1)}), bf16[256,2048]{0,1:T(8,128)(2,1)}) %reduce-scatter.7.cloned.1.call-update) | async-done | bytes 1048592 | tf_op jit(solution)/shard_map/reduce_scatter | solution.py:43
  233.4 1.7 fusion.3
  235.1 8.0 %all-reduce.2 = (f32[256]{0:T(256)S(1)}, f32[256]{0:T(256)S(1)}) all-reduce(f32[256]{0:T(256)S(1)} %get-tuple-element.23, f32[256]{0:T(256)S(1)} %get-tuple-element.21), channel_id=1, replica_groups=mesh['dp'=8,'mp'=4] {'mp'}, use_global_device_ids=true, to_apply=%region_9.0 | all-reduce | flops 512 | bytes 4096 | tf_op jit(solution)/shard_map/psum | solution.py:69
  245.0 78.7 %reduce-scatter.11.cloned.1.call-done = bf16[256,2048]{1,0:T(8,128)(2,1)} async-done(((bf16[2048,2048]{1,0:T(8,128)(2,1)}), bf16[256,2048]{1,0:T(8,128)(2,1)}) %reduce-scatter.11.cloned.1.call-update) | async-done | bytes 1048592 | tf_op jit(solution)/shard_map/reduce_scatter | solution.py:52
  323.7 1.6 fusion.7
  325.9 0.7 pad_maximum_fusion
  326.6 43.2 %all-reduce = (f32[3]{0:T(128)S(1)}, f32[2048]{0:T(1024)S(1)}) all-reduce(f32[3]{0:T(128)S(1)} %pad_maximum_fusion, f32[2048]{0:T(1024)S(1)} %get-tuple-element.24), channel_id=1, replica_groups=mesh['dp'=8,'mp'=4] {'dp','mp'}, use_global_device_ids=true, to_apply=%region_14.0 | all-reduce | flops 2051 | bytes 16408 | tf_op jit(solution)/shard_map/psum | solution.py:85
  369.9 21.0 %all-reduce.1 = (f32[2048]{0:T(1024)S(1)}, f32[2048]{0:T(1024)S(1)}) all-reduce(f32[2048]{0:T(1024)S(1)} %get-tuple-element.22, f32[2048]{0:T(1024)S(1)} %get-tuple-element.20), channel_id=1, replica_groups=mesh['dp'=8,'mp'=4] {'dp'}, use_global_device_ids=true, to_apply=%region_17.0 | all-reduce | flops 4096 | bytes 32768 | tf_op jit(solution)/shard_map/psum | solution.py:70
  390.9 0.6 fusion.15
  391.6 3.1 multiply_reduce_fusion
  394.7 2.1 multiply_reduce_fusion.1
  396.8 2.1 multiply_reduce_fusion.2
  398.9 2.0 pad_maximum_fusion.1
  400.9 43.5 %psum.55 = f32[3]{0:T(128)S(1)} all-reduce(f32[3]{0:T(128)S(1)} %pad_maximum_fusion.1), channel_id=1, replica_groups=mesh['dp'=8,'mp'=4] {'dp','mp'}, use_global_device_ids=true, to_apply=%region_22.0 | all-reduce | flops 3 | bytes 24 | tf_op jit(solution)/shard_map/psum | solution.py:90
  444.4 0.7 fusion.14
  445.1 1.8 broadcast_divide_fusion.1
  446.9 1.8 copy.23
  448.7 4.6 broadcast_divide_fusion.2
  453.3 2.9 copy.22
  456.2 4.3 broadcast_divide_fusion
  (55 shorter events, 1.6 us)
Async XLA Ops:
  7.2 1.9 copy-start
  7.2 135.9 %reduce-scatter.9.cloned.1.call-start = ((), (), s32[]{:S(2)}) async-start(), calls=%async_computation.6 | async-start | bytes 9437184 | tf_op jit(solution)/shard_map/reduce_scatter | solution.py:49
  9.1 10.8 %copy-start.16 = (bf16[2048,2048]{1,0:T(8,128)(2,1)S(1)}, bf16[2048,2048]{1,0:T(8,128)(2,1)}, u32[]{:S(2)}) copy-start(bf16[2048,2048]{1,0:T(8,128)(2,1)} %param.15) | copy-start | bytes 25165828
  19.9 8.7 %copy-start.17 = (bf16[768,2048]{1,0:T(8,128)(2,1)S(1)}, bf16[768,2048]{1,0:T(8,128)(2,1)}, u32[]{:S(2)}) copy-start(bf16[768,2048]{1,0:T(8,128)(2,1)} %param.13) | copy-start | bytes 9437188
  55.0 178.4 %reduce-scatter.7.cloned.1.call-start = ((), (), s32[]{:S(2)}) async-start(), calls=%async_computation.5 | async-start | bytes 9437184 | tf_op jit(solution)/shard_map/reduce_scatter | solution.py:43
  66.0 1.9 copy-start.18
  66.0 257.7 %reduce-scatter.11.cloned.1.call-start = ((), (), s32[]{:S(2)}) async-start(), calls=%async_computation.7 | async-start | bytes 9437184 | tf_op jit(solution)/shard_map/reduce_scatter | solution.py:52
  82.6 10.6 %copy-start.20 = (bf16[768,2048]{1,0:T(8,128)(2,1)S(1)}, bf16[768,2048]{1,0:T(8,128)(2,1)}, u32[]{:S(2)}) copy-start(bf16[768,2048]{1,0:T(8,128)(2,1)} %get-tuple-element.38) | copy-start | bytes 9437188
  82.6 377.9 %reduce-scatter.5.cloned.1.call-start = ((), (), s32[]{:S(2)}) async-start(), calls=%async_computation.4 | async-start | bytes 3932160 | tf_op jit(solution)/shard_map/reduce_scatter | solution.py:63
  103.6 139.5 %copy-start.13 = (f32[256]{0:T(256)S(1)}, f32[256]{0:T(256)}, u32[]{:S(2)}) copy-start(f32[256]{0:T(256)} %param.17) | copy-start | bytes 3076
  103.6 139.5 %copy-start.14 = (f32[256]{0:T(256)S(1)}, f32[256]{0:T(256)}, u32[]{:S(2)}) copy-start(f32[256]{0:T(256)} %param.19) | copy-start | bytes 3076
  103.6 221.7 %copy-start.15 = (f32[256]{0:T(256)S(1)}, f32[256]{0:T(256)}, u32[]{:S(2)}) copy-start(f32[256]{0:T(256)} %param.21) | copy-start | bytes 3076
  103.6 266.2 %copy-start.19 = (f32[3]{0:T(128)S(1)}, f32[3]{0:T(128)}, u32[]{:S(2)}) copy-start(f32[3]{0:T(128)} %constant.38) | copy-start | bytes 40
  103.6 287.9 %copy-start.10 = (f32[2048]{0:T(1024)S(1)}, f32[2048]{0:T(1024)}, u32[]{:S(2)}) copy-start(f32[2048]{0:T(1024)} %param.22) | copy-start | bytes 24580
  103.6 287.9 %copy-start.11 = (f32[2048]{0:T(1024)S(1)}, f32[2048]{0:T(1024)}, u32[]{:S(2)}) copy-start(f32[2048]{0:T(1024)} %param.20) | copy-start | bytes 24580
  103.6 287.9 %copy-start.12 = (f32[2048]{0:T(1024)S(1)}, f32[2048]{0:T(1024)}, u32[]{:S(2)}) copy-start(f32[2048]{0:T(1024)} %param.18) | copy-start | bytes 24580
  143.1 251.6 %copy-start.2 = (bf16[256,2048]{0,1:T(8,128)(2,1)S(1)}, bf16[256,2048]{0,1:T(8,128)(2,1)}, u32[]{:S(2)}) copy-start(bf16[256,2048]{0,1:T(8,128)(2,1)} %reduce-scatter.9.cloned.1.call-done) | copy-start | bytes 3145732
  233.4 163.4 %copy-start.3 = (bf16[256,2048]{0,1:T(8,128)(2,1)S(1)}, bf16[256,2048]{0,1:T(8,128)(2,1)}, u32[]{:S(2)}) copy-start(bf16[256,2048]{0,1:T(8,128)(2,1)} %reduce-scatter.7.cloned.1.call-done) | copy-start | bytes 3145732
  243.7 203.1 %copy-start.8 = (f32[256]{0:T(256)}, f32[256]{0:T(256)S(1)}, u32[]{:S(2)}) copy-start(f32[256]{0:T(256)S(1)} %get-tuple-element.47) | copy-start | bytes 3076
  243.7 205.0 %copy-start.7 = (f32[256]{0:T(256)}, f32[256]{0:T(256)S(1)}, u32[]{:S(2)}) copy-start(f32[256]{0:T(256)S(1)} %get-tuple-element.33) | copy-start | bytes 3076
  325.9 130.3 %copy-start.9 = (f32[256]{0:T(256)}, f32[256]{0:T(256)S(1)}, u32[]{:S(2)}) copy-start(f32[256]{0:T(256)S(1)} %get-tuple-element.37) | copy-start | bytes 3076
  391.5 64.7 %copy-start.4 = (f32[2048]{0:T(1024)}, f32[2048]{0:T(1024)S(1)}, u32[]{:S(2)}) copy-start(f32[2048]{0:T(1024)S(1)} %multiply_add_fusion) | copy-start | bytes 24580
  391.6 55.3 %copy-start.5 = (f32[2048]{0:T(1024)}, f32[2048]{0:T(1024)S(1)}, u32[]{:S(2)}) copy-start(f32[2048]{0:T(1024)S(1)} %get-tuple-element.48) | copy-start | bytes 24580
  391.6 57.1 %copy-start.6 = (f32[2048]{0:T(1024)}, f32[2048]{0:T(1024)S(1)}, u32[]{:S(2)}) copy-start(f32[2048]{0:T(1024)S(1)} %get-tuple-element.49) | copy-start | bytes 24580
  448.7 11.8 %copy-start.1 = (bf16[768,2048]{1,0:T(8,128)(2,1)S(1)}, bf16[768,2048]{1,0:T(8,128)(2,1)}, u32[]{:S(2)}) copy-start(bf16[768,2048]{1,0:T(8,128)(2,1)} %param.12) | copy-start | bytes 9437188
Sparse Core Ops, SparseCore 0:
  55.1 87.9 reduce-scatter.8
  145.4 87.9 reduce-scatter.6
  235.7 87.9 reduce-scatter.10
  327.1 45.7 reduce-scatter.4
where the time goes:
time: 468 us; the launch traced here: 467 us
  waiting for transfers between devices  207 us (44%)
  blocking collectives  116 us (25%)
  matrix products  92.4 us (20%)
  other arithmetic  26.9 us (6%)
  between operations  15.2 us (3%)
  local copies, waits for them, and re-layouts  9.81 us (2%)
    reduce_scatter x1, waiting for transfers between devices, body(): lax.psum_scatter(weight_term(tokens, grad_gate).astype(jnp.bfloat16), 'dp...  88.6 us
    reduce_scatter x1, waiting for transfers between devices, body(): lax.psum_scatter(weight_term(hidden, cotangent).astype(jnp.bfloat16), 'dp...  78.7 us
    psum x1, blocking collectives, body(): lax.psum(jnp.stack([jnp.sum(raw_gate * raw_gate), jnp.sum(raw_up * raw_up...  43.5 us
    psum x1, blocking collectives, body(): row_means = lax.psum(new_sums, ('dp', 'mp')) / row_counts  43.2 us
    reduce_scatter x1, waiting for transfers between devices, body(): lax.psum_scatter(weight_term(tokens, grad_up).astype(jnp.bfloat16), 'dp',...  39.5 us
    dot_general x3, matrix products, weight_term(): jnp.einsum('tr,tc->rc', left_side, right_side, preferred_element_type=jnp...  36.5 us
    psum x1, blocking collectives, body(): lax.psum((jnp.sum(squares_gate, 0), jnp.sum(squares_up, 0)), 'dp')  21 us
    dot_general x1, matrix products, body(): jnp.einsum('td,fd->tf', cotangent, w_down, preferred_element_type=jnp.flo...  15.5 us
  transfers between devices with their start and end apart: 4, of which 3 were waited for; matrix products, arithmetic and copies ran while one was open for 17% of the time, Pallas kernels for 0%

commit v1 on v0

v1 whole, which is shorter than its diff:
```python
import functools

import jax
import jax.numpy as jnp
from jax import lax
from jax.experimental import pallas as pl
from jax.experimental.pallas import tpu as pltpu
from jax.sharding import PartitionSpec as P

epsilon_one = 1e-30
decay_rate = 0.8
MESH = pl.DeviceIdType.MESH


def silu_parts(gate_pre):
    sig = jax.nn.sigmoid(gate_pre)
    return (gate_pre * sig, sig * (1.0 + gate_pre * (1.0 - sig)))


def moment_step(old_value, column_total, count):
    return decay_rate * old_value + (1.0 - decay_rate) * (column_total / count + epsilon_one)


def exchange_kernel(
    n_dp, n_mp, tail, dp_ref, mp_ref, dp_out, mp_out, dp_slots, mp_slots, d_send, d_recv, m_send, m_recv
):
    d = lax.axis_index("dp")
    m = lax.axis_index("mp")
    barrier = pltpu.get_barrier_semaphore()
    for k in range(1, n_dp):
        pl.semaphore_signal(
            barrier, inc=1, device_id=(lax.rem(d + k, n_dp), m), device_id_type=MESH
        )
    for k in range(1, n_mp):
        pl.semaphore_signal(
            barrier, inc=1, device_id=(d, lax.rem(m + k, n_mp)), device_id_type=MESH
        )
    pl.semaphore_wait(barrier, n_dp + n_mp - 2)

    dp_slots[0] = dp_ref[...]
    copies = []
    for k in range(1, n_dp):
        copies.append(
            pltpu.make_async_remote_copy(
                src_ref=dp_ref,
                dst_ref=dp_slots.at[k],
                send_sem=d_send.at[k],
                recv_sem=d_recv.at[k],
                device_id=(lax.rem(d + k, n_dp), m),
                device_id_type=MESH,
            )
        )
        copies[-1].start()
    for copy in copies:
        copy.wait()
    total = dp_slots[d]
    for j in range(1, n_dp):
        total = total + dp_slots[lax.rem(d - j + n_dp, n_dp)]
    dp_out[...] = total

    own_rows = mp_ref.shape[0]
    mp_slots[0, :own_rows] = mp_ref[...]
    mp_slots[0, own_rows:] = total[tail:]
    copies = []
    for k in range(1, n_mp):
        copies.append(
            pltpu.make_async_remote_copy(
                src_ref=mp_slots.at[0],
                dst_ref=mp_slots.at[k],
                send_sem=m_send.at[k],
                recv_sem=m_recv.at[k],
                device_id=(d, lax.rem(m + k, n_mp)),
                device_id_type=MESH,
            )
        )
        copies[-1].start()
    for copy in copies:
        copy.wait()
    total = mp_slots[m]
    for j in range(1, n_mp):
        total = total + mp_slots[lax.rem(m - j + n_mp, n_mp)]
    mp_out[...] = total


def exchange(dp_part, mp_part, tail, collective_id):
    n_dp, n_mp = lax.axis_size("dp"), lax.axis_size("mp")
    mp_rows = mp_part.shape[0] + dp_part.shape[0] - tail
    vmem = pl.BlockSpec(memory_space=pltpu.VMEM)
    return pl.pallas_call(
        functools.partial(exchange_kernel, n_dp, n_mp, tail),
        out_shape=(
            jax.ShapeDtypeStruct(dp_part.shape, jnp.float32),
            jax.ShapeDtypeStruct((mp_rows, 128), jnp.float32),
        ),
        in_specs=[vmem, vmem],
        out_specs=(vmem, vmem),
        scratch_shapes=[
            pltpu.VMEM((n_dp,) + dp_part.shape, jnp.float32),
            pltpu.VMEM((n_mp, mp_rows, 128), jnp.float32),
            pltpu.SemaphoreType.DMA((n_dp,)),
            pltpu.SemaphoreType.DMA((n_dp,)),
            pltpu.SemaphoreType.DMA((n_mp,)),
            pltpu.SemaphoreType.DMA((n_mp,)),
        ],
        compiler_params=pltpu.CompilerParams(
            collective_id=collective_id, has_side_effects=True, vmem_limit_bytes=8 * 2**20
        ),
    )(dp_part, mp_part)


def pack(*parts):
    flat = jnp.concatenate([part.reshape(-1) for part in parts])
    pad = -flat.shape[0] % 1024
    return jnp.pad(flat, (0, pad)).reshape(-1, 128)


def chain_scatter(blocks):
    n_dp = lax.axis_size("dp")
    count = n_dp // 2
    p = lax.axis_index("dp") // 2

    def pick(index):
        return lax.dynamic_index_in_dim(blocks, jnp.clip(index, 0, count - 1), 0, keepdims=False)

    from_left = from_right = None
    for step in range(1, count):
        to_right, to_left = pick(count - step + p), pick(step - count + p)
        if step > 1:
            to_right, to_left = to_right + from_left, to_left + from_right
        right_pairs = [
            (2 * q + c, 2 * q + 2 + c) for q in range(step) for c in range(2)
        ]
        left_pairs = [
            (2 * q + c, 2 * q - 2 + c)
            for q in range(count - step, count)
            for c in range(2)
        ]
        from_left = lax.ppermute(to_right, "dp", right_pairs)
        from_right = lax.ppermute(to_left, "dp", left_pairs)
    own = pick(p).astype(jnp.float32)
    return own + from_left.astype(jnp.float32) + from_right.astype(jnp.float32)


def body(
    tokens, cotangent, w_gate, w_up, w_down, row_gate, col_gate, row_up, col_up, row_down, col_down
):
    data_count = lax.axis_size("dp")
    model_count = lax.axis_size("mp")
    tok_rows, width_model = tokens.shape
    units = w_gate.shape[1]
    all_units = units * model_count
    grad_scale = float(tok_rows * data_count) ** (-0.5)
    core = lax.axis_index("dp") % 2
    swap = [(i, i ^ 1) for i in range(data_count)]
    chain = data_count // 2

    def halves(left_side):
        shaped = left_side.reshape(tok_rows, chain, 2, -1)

        def half(which):
            part = lax.dynamic_index_in_dim(shaped, which, 2, keepdims=False)
            return part.reshape(tok_rows, -1)

        return half(1 - core), half(core)

    def weight_term(left_side, right_side):
        return (
            jnp.einsum("tr,tc->rc", left_side, right_side, preferred_element_type=jnp.float32)
            * grad_scale
        ).astype(jnp.bfloat16)

    def pair_sum(parts, right_side):
        other, own = parts
        theirs = weight_term(other, right_side)
        received = lax.ppermute(theirs, "dp", swap)
        mine = weight_term(own, right_side)
        total = mine + received
        return theirs, mine, total.reshape(chain, -1, total.shape[1])

    gate_pre = jnp.dot(tokens, w_gate, preferred_element_type=jnp.float32)
    up_pre = jnp.dot(tokens, w_up, preferred_element_type=jnp.float32)
    activated, derivative = silu_parts(gate_pre)
    hidden = (activated * up_pre).astype(jnp.bfloat16)
    theirs, mine, blocks_down = pair_sum(halves(hidden), cotangent)
    cotangent_late, _, _ = lax.optimization_barrier((cotangent, theirs, mine))
    hidden_grad = jnp.einsum(
        "td,fd->tf", cotangent_late, w_down, preferred_element_type=jnp.float32
    )
    grad_gate = (hidden_grad * up_pre * derivative).astype(jnp.bfloat16)
    grad_up = (hidden_grad * activated).astype(jnp.bfloat16)
    token_halves = halves(tokens)
    theirs_g, mine_g, blocks_gate = pair_sum(token_halves, grad_gate)
    theirs_u, mine_u, blocks_up = pair_sum(token_halves, grad_up)
    grad_gate_late, grad_up_late, _, _, _, _ = lax.optimization_barrier(
        (grad_gate, grad_up, theirs_g, mine_g, theirs_u, mine_u)
    )
    input_terms = jnp.einsum("tf,df->td", grad_gate_late, w_gate, preferred_element_type=jnp.float32)
    input_terms = input_terms + jnp.einsum(
        "tf,df->td", grad_up_late, w_up, preferred_element_type=jnp.float32
    )
    token_grad = lax.psum_scatter(
        input_terms.astype(jnp.bfloat16), "mp", scatter_dimension=1, tiled=True
    )
    g_down = chain_scatter(blocks_down)
    g_gate = chain_scatter(blocks_gate)
    g_up = chain_scatter(blocks_up)

    squares_gate = g_gate * g_gate
    squares_up = g_up * g_up
    squares_down = g_down * g_down
    rows_gate, rows_up = jnp.sum(squares_gate, 1), jnp.sum(squares_up, 1)
    row_down_new = moment_step(row_down, jnp.sum(squares_down, 1), width_model)
    row_local = row_gate.shape[0]

    def new_row_share(row_old, row_part):
        old = decay_rate * jnp.sum(row_old) / model_count
        return old + (1.0 - decay_rate) * (
            jnp.sum(row_part) / all_units + row_local * epsilon_one / model_count
        )

    shares = jnp.stack(
        [new_row_share(row_gate, rows_gate), new_row_share(row_up, rows_up), jnp.sum(row_down_new)]
    )
    dp_part = pack(
        jnp.sum(squares_gate, 0), jnp.sum(squares_up, 0), jnp.sum(squares_down, 0), shares
    )
    mp_part = pack(rows_gate, rows_up)
    tail = 2 * units // 128
    dp_sum, mp_sum = exchange(dp_part, mp_part, tail, 0)
    col_sums = dp_sum[:tail].reshape(2, units)
    row_sums = mp_sum[: mp_part.shape[0]].reshape(-1)
    both = mp_sum[mp_part.shape[0] :].reshape(-1)
    row_counts = jnp.array([width_model, width_model, all_units], jnp.float32)
    row_means = both[width_model : width_model + 3] / row_counts
    row_gate_new = moment_step(row_gate, row_sums[:row_local], all_units)
    row_up_new = moment_step(row_up, row_sums[row_local : 2 * row_local], all_units)
    col_gate_new = moment_step(col_gate, col_sums[0], width_model)
    col_up_new = moment_step(col_up, col_sums[1], width_model)
    col_down_new = moment_step(col_down, both[:width_model], all_units)

    def raw_of(grad, row_new, col_new, row_mean):
        return grad * lax.rsqrt(row_new / row_mean)[:, None] * lax.rsqrt(col_new)[None, :]

    raw_gate = raw_of(g_gate, row_gate_new, col_gate_new, row_means[0])
    raw_up = raw_of(g_up, row_up_new, col_up_new, row_means[1])
    raw_down = raw_of(g_down, row_down_new, col_down_new, row_means[2])
    raw_parts = jnp.stack(
        [jnp.sum(raw_gate * raw_gate), jnp.sum(raw_up * raw_up), jnp.sum(raw_down * raw_down)]
    )
    _, raw_sum = exchange(pack(raw_parts), jnp.zeros((8, 128), jnp.float32), 0, 1)
    raw_totals = raw_sum[8, :3]
    divisor = jnp.maximum(1.0, jnp.sqrt(raw_totals / float(width_model * all_units)))
    update_gate = raw_gate / divisor[0]
    update_up = raw_up / divisor[1]
    update_down = raw_down / divisor[2]
    return (
        token_grad,
        update_gate,
        update_up,
        update_down,
        row_gate_new,
        col_gate_new,
        row_up_new,
        col_up_new,
        row_down_new,
        col_down_new,
    )


def solution(mesh):
    in_specs = (
        P("dp", None),
        P("dp", None),
        P(None, "mp"),
        P(None, "mp"),
        P("mp", None),
        P("dp"),
        P("mp"),
        P("dp"),
        P("mp"),
        P(("mp", "dp")),
        P(),
    )
    out_specs = (
        P("dp", "mp"),
        P("dp", "mp"),
        P("dp", "mp"),
        P(("mp", "dp"), None),
        P("dp"),
        P("mp"),
        P("dp"),
        P("mp"),
        P(("mp", "dp")),
        P(),
    )
    return jax.shard_map(body, mesh=mesh, in_specs=in_specs, out_specs=out_specs, check_vma=False)
```

time: 468 us -> 430 us (0.919); the launches traced: 467 us -> 422 us
  blocking collectives: 116 us -> 0 us
  waiting for transfers between devices: 207 us -> 145 us
  local copies, waits for them, and re-layouts: 9.81 us -> 53.5 us
  starting transfers between devices: 0.16 us -> 37.6 us
  other arithmetic: 26.9 us -> 51.6 us
  Pallas kernels: 0 us -> 20.3 us
    reduce_scatter x3 -> x0, waiting for transfers between devices: 207 us -> none  [the longest x1 88.6 us: body(): lax.psum_scatter(weight_term(tokens, grad_gate).astype(jnp.bfloat16), 'dp...]
    ppermute x0 -> x21, waiting for transfers between devices: none -> 145 us  [the longest x9 118 us: chain_scatter(): from_left = lax.ppermute(to_right, 'dp', right_pairs)]
    psum x4 -> x0, blocking collectives: 116 us -> none  [the longest x1 43.5 us: body(): lax.psum(jnp.stack([jnp.sum(raw_gate * raw_gate), jnp.sum(raw_up * raw_up...]
    ppermute x0 -> x21, starting transfers between devices: none -> 37.6 us  [the longest x9 22.1 us: chain_scatter(): from_left = lax.ppermute(to_right, 'dp', right_pairs)]
    add x2 -> x9, other arithmetic: 0.02 us -> 20.5 us  [chain_scatter(): to_right, to_left = (to_right + from_left, to_left + from_right)]
    pallas_call x0 -> x2, Pallas kernels: none -> 20.3 us  [exchange(): pl.pallas_call(functools.partial(exchange_kernel, n_dp, n_mp, tail), out_...]
    unnamed x44 -> x67, local copies, waits for them, and re-layouts: 8.5 us -> 24.1 us
    dynamic_slice x0 -> x2, local copies, waits for them, and re-layouts: none -> 15.3 us  [half(): part = lax.dynamic_index_in_dim(shaped, which, 2, keepdims=False)]
  transfers between devices with their start and end apart: 4 -> 22, of which waited for: 3 -> 11; matrix products, arithmetic and copies ran while one was open for 17% -> 27% of each run, Pallas kernels for 0% -> 5%
where the time goes in v1:
time: 430 us; the launch traced here: 422 us
  waiting for transfers between devices  145 us (34%)
  matrix products  96.7 us (22%)
  local copies, waits for them, and re-layouts  53.5 us (12%)
  other arithmetic  51.6 us (12%)
  starting transfers between devices  37.6 us (9%)
  Pallas kernels  20.3 us (5%)
  between operations  17.5 us (4%)
    ppermute x9, waiting for transfers between devices, chain_scatter(): from_left = lax.ppermute(to_right, 'dp', right_pairs)  118 us
    dot_general x6, matrix products, weight_term(): jnp.einsum('tr,tc->rc', left_side, right_side, preferred_element_type=jnp...  37.9 us
    ppermute x9, waiting for transfers between devices, chain_scatter(): from_right = lax.ppermute(to_left, 'dp', left_pairs)  27 us
    unnamed x67, local copies, waits for them, and re-layouts  24.1 us
    ppermute x9, starting transfers between devices, chain_scatter(): from_left = lax.ppermute(to_right, 'dp', right_pairs)  22.1 us
    add x9, other arithmetic, chain_scatter(): to_right, to_left = (to_right + from_left, to_left + from_right)  20.5 us
    pallas_call x2, Pallas kernels, exchange(): pl.pallas_call(functools.partial(exchange_kernel, n_dp, n_mp, tail), out_...  20.3 us
    dot_general x1, matrix products, body(): jnp.einsum('td,fd->tf', cotangent_late, w_down, preferred_element_type=jn...  15.5 us
  transfers between devices with their start and end apart: 22, of which 11 were waited for; matrix products, arithmetic and copies ran while one was open for 27% of the time, Pallas kernels for 5%

profile of v1, /device:TPU:10, one launch (start us, length us, event | category | flops | bytes accessed | tf_op | source)
XLA Modules:
  0.0 421.9 jit_solution(15657655202243637323)
XLA Ops:
  7.3 11.0 %fusion.20 = f32[768,2048]{1,0:T(8,128)S(1)} fusion(bf16[768,2048]{1,0:T(8,128)(2,1)} %param.12, bf16[2048,2048]{1,0:T(8,128)(2,1)} %param.14), kind=kOutput, calls=%fused_computation.86 | convolution fusion | flops 6442450944 | bytes 17825792 | tf_op jit(solution)/shard_map/dot_general | solution.py:180
  18.3 9.3 %multiply_convert_fusion.8 = (bf16[768,2048]{1,0:T(8,128)(2,1)}, f32[768,2048]{1,0:T(8,128)}) fusion(f32[768,2048]{1,0:T(8,128)S(1)} %fusion.20, bf16[768,2048]{1,0:T(8,128)(2,1)S(1)} %copy-done.12, bf16[2048,2048]{1,0:T(8,128)(2,1)S(1)} %copy-done.25), kind=kOutput, calls=%fused_computation.9 | convolution fusion | flops 6451888128 | bytes 27262976 | tf_op jit(solution)/shard_map/dot_general | solution.py:181
  27.6 6.7 %reshape.125 = bf16[768,4,2,256]{3,2,1,0:T(2,128)(2,1)} reshape(bf16[768,2048]{1,0:T(8,128)(2,1)} %get-tuple-element.72) | data formatting | bytes 6291456 | tf_op jit(solution)/shard_map/reshape | solution.py:158
  34.3 11.9 %constant_dynamic-slice_fusion.2 = (bf16[768,4,1,256]{3,2,1,0:T(2,128)(2,1)}, bf16[768,4,1,256]{3,2,1,0:T(2,128)(2,1)}) fusion(bf16[768,4,2,256]{3,2,1,0:T(2,128)(2,1)} %reshape.125, s32[]{:T(128)S(6)} %select_n.46, s32[]{:T(128)S(6)} %select_n.45), kind=kLoop, calls=%fused_computation.60 | loop fusion | bytes 6291464 | tf_op jit(solution)/shard_map/jit(dynamic_index_in_dim)/dynamic_slice | solution.py:161
  46.3 8.1 %copy.27 = bf16[768,4,1,256]{0,3,1,2:T(8,128)(2,1)} copy(bf16[768,4,1,256]{3,2,1,0:T(2,128)(2,1)} %get-tuple-element.61) | data formatting | bytes 3145728
  54.4 6.4 %multiply_convert_fusion.5 = bf16[1024,2048]{1,0:T(8,128)(2,1)} fusion(bf16[768,1024]{0,1:T(8,128)(2,1)} %bitcast.139, bf16[768,2048]{1,0:T(8,128)(2,1)S(1)} %copy-done), kind=kOutput, calls=%fused_computation.5 | convolution fusion | flops 3225419776 | bytes 8912896 | tf_op jit(solution)/shard_map/tr,tc->rc/dot_general | solution.py:168
  60.7 4.7 %copy.26 = bf16[768,2048]{0,1:T(8,128)(2,1)} copy(bf16[768,2048]{1,0:T(8,128)(2,1)} %param.12) | data formatting | bytes 6291456 | tf_op args[0]
  65.5 8.1 %copy.28 = bf16[768,4,1,256]{0,3,1,2:T(8,128)(2,1)} copy(bf16[768,4,1,256]{3,2,1,0:T(2,128)(2,1)} %get-tuple-element.60) | data formatting | bytes 3145728
  77.0 7.2 %fusion.19 = bf16[1024,2048]{1,0:T(8,128)(2,1)} fusion(bf16[1024,2048]{1,0:T(8,128)(2,1)} %collective-permute-done.14, bf16[768,1024]{0,1:T(8,128)(2,1)S(1)} %bitcast.138, bf16[768,2048]{1,0:T(8,128)(2,1)S(1)} %copy-done), kind=kOutput, calls=%fused_computation.85 | convolution fusion | flops 3227516928 | bytes 13107200 | tf_op jit(solution)/shard_map/tr,tc->rc/dot_general | solution.py:168
  84.2 15.5 %multiply_convert_fusion.6 = (bf16[768,2048]{1,0:T(8,128)(2,1)}, bf16[768,2048]{1,0:T(8,128)(2,1)}) fusion(f32[768,2048]{1,0:T(8,128)} %copy-done.29, f32[768,2048]{1,0:T(8,128)} %get-tuple-element.73, bf16[768,2048]{1,0:T(8,128)(2,1)S(1)} %copy-done, bf16[2048,2048]{1,0:T(8,128)(2,1)} %param.16), kind=kOutput, calls=%fused_computation.7 | convolution fusion | flops 6462898176 | bytes 30408704 | tf_op jit(solution)/shard_map/td,fd->tf/dot_general | solution.py:186
  99.7 7.0 %multiply_convert_fusion.1 = bf16[1024,2048]{1,0:T(8,128)(2,1)} fusion(bf16[768,1024]{0,1:T(8,128)(2,1)S(1)} %bitcast.142, bf16[768,2048]{1,0:T(8,128)(2,1)} %get-tuple-element.18), kind=kOutput, calls=%fused_computation.1 | convolution fusion | flops 3225419776 | bytes 8912896 | tf_op jit(solution)/shard_map/tr,tc->rc/dot_general | solution.py:168
  111.3 6.8 %multiply_convert_fusion.3 = bf16[1024,2048]{1,0:T(8,128)(2,1)} fusion(bf16[768,1024]{0,1:T(8,128)(2,1)S(1)} %bitcast.143, bf16[768,2048]{1,0:T(8,128)(2,1)} %get-tuple-element.17), kind=kOutput, calls=%fused_computation.3 | convolution fusion | flops 3225419776 | bytes 8912896 | tf_op jit(solution)/shard_map/tr,tc->rc/dot_general | solution.py:168
  119.9 17.5 %collective-permute-done.15 = bf16[256,2048]{1,0:T(8,128)(2,1)} collective-permute-done((bf16[256,2048]{1,0:T(8,128)(2,1)}, bf16[256,2048]{1,0:T(8,128)(2,1)}, u32[]{:S(2)}, u32[]{:S(2)}) %collective-permute-start.15) | collective-permute-done | bytes 1048608 | tf_op jit(solution)/shard_map/ppermute | solution.py:138
  141.9 24.6 %collective-permute-done.16 = bf16[256,2048]{1,0:T(8,128)(2,1)} collective-permute-done((bf16[256,2048]{1,0:T(8,128)(2,1)}, bf16[256,2048]{1,0:T(8,128)(2,1)}, u32[]{:S(2)}, u32[]{:S(2)}) %collective-permute-start.16) | collective-permute-done | bytes 1048608 | tf_op jit(solution)/shard_map/ppermute | solution.py:138
  166.5 3.7 bitcast_add_fusion.3
  171.6 5.2 %fusion.18 = bf16[1024,2048]{1,0:T(8,128)(2,1)S(1)} fusion(bf16[1024,2048]{1,0:T(8,128)(2,1)} %collective-permute-done.7, bf16[768,1024]{0,1:T(8,128)(2,1)S(1)} %bitcast.140, bf16[768,2048]{1,0:T(8,128)(2,1)S(1)} %copy-done.27), kind=kOutput, calls=%fused_computation.84 | convolution fusion | flops 3227516928 | bytes 13107200 | tf_op jit(solution)/shard_map/tr,tc->rc/dot_general | solution.py:168
  181.0 5.2 %fusion.17 = bf16[1024,2048]{1,0:T(8,128)(2,1)S(1)} fusion(bf16[1024,2048]{1,0:T(8,128)(2,1)} %collective-permute-done, bf16[768,1024]{0,1:T(8,128)(2,1)S(1)} %bitcast.141, bf16[768,2048]{1,0:T(8,128)(2,1)S(1)} %copy-done.28), kind=kOutput, calls=%fused_computation.83 | convolution fusion | flops 3227516928 | bytes 13107200 | tf_op jit(solution)/shard_map/tr,tc->rc/dot_general | solution.py:168
  190.7 5.2 %collective-permute-start.17 = (bf16[256,2048]{1,0:T(8,128)(2,1)}, bf16[256,2048]{1,0:T(8,128)(2,1)S(1)}, u32[]{:S(2)}, u32[]{:S(2)}) collective-permute-start(bf16[256,2048]{1,0:T(8,128)(2,1)} %get-tuple-element.46), channel_id=1, source_target_pairs={{0,8},{4,12},{8,16},{12,20},{16,24},{20,28},{1,9},{5,13},{9,17},{1... | collective-permute-start | bytes 3145736 | tf_op jit(solution)/shard_map/ppermute | solution.py:138
  200.0 7.0 %collective-permute-done.8 = bf16[256,2048]{1,0:T(8,128)(2,1)} collective-permute-done((bf16[256,2048]{1,0:T(8,128)(2,1)}, bf16[256,2048]{1,0:T(8,128)(2,1)}, u32[]{:S(2)}, u32[]{:S(2)}) %collective-permute-start.8) | collective-permute-done | bytes 1048608 | tf_op jit(solution)/shard_map/ppermute | solution.py:138
  210.8 18.6 %collective-permute-done.1 = bf16[256,2048]{1,0:T(8,128)(2,1)} collective-permute-done((bf16[256,2048]{1,0:T(8,128)(2,1)}, bf16[256,2048]{1,0:T(8,128)(2,1)}, u32[]{:S(2)}, u32[]{:S(2)}) %collective-permute-start.1) | collective-permute-done | bytes 1048608 | tf_op jit(solution)/shard_map/ppermute | solution.py:138
  233.1 11.9 %fusion.21 = f32[768,2048]{1,0:T(8,128)} fusion(bf16[768,2048]{1,0:T(8,128)(2,1)} %get-tuple-element.17, bf16[2048,2048]{1,0:T(8,128)(2,1)} %param.14), kind=kOutput, calls=%fused_computation.87 | convolution fusion | flops 6442450944 | bytes 17825792 | tf_op jit(solution)/shard_map/tf,df->td/dot_general | solution.py:197
  245.0 3.8 collective-permute-start.20
  248.9 25.4 %collective-permute-done.9 = bf16[256,2048]{1,0:T(8,128)(2,1)S(1)} collective-permute-done((bf16[256,2048]{1,0:T(8,128)(2,1)S(1)}, bf16[256,2048]{1,0:T(8,128)(2,1)S(1)}, u32[]{:S(2)}, u32[]{:S(2)}) %collective-permute-start.9) | collective-permute-done | bytes 1048608 | tf_op jit(solution)/shard_map/ppermute | solution.py:138
  277.1 17.0 %collective-permute-done.2 = bf16[256,2048]{1,0:T(8,128)(2,1)S(1)} collective-permute-done((bf16[256,2048]{1,0:T(8,128)(2,1)S(1)}, bf16[256,2048]{1,0:T(8,128)(2,1)S(1)}, u32[]{:S(2)}, u32[]{:S(2)}) %collective-permute-start.2) | collective-permute-done | bytes 1048608 | tf_op jit(solution)/shard_map/ppermute | solution.py:138
  296.9 11.1 %add_convert_fusion = bf16[768,2048]{1,0:T(8,128)(2,1)} fusion(f32[768,2048]{1,0:T(8,128)} %fusion.21, bf16[768,2048]{1,0:T(8,128)(2,1)} %get-tuple-element.18, bf16[2048,2048]{1,0:T(8,128)(2,1)S(1)} %bitcast.145), kind=kOutput, calls=%fused_computation.6 | convolution fusion | flops 6445596672 | bytes 20971520 | tf_op jit(solution)/shard_map/tf,df->td/dot_general | solution.py:198
  308.0 4.6 %collective-permute-start.10 = (bf16[256,2048]{1,0:T(8,128)(2,1)}, bf16[256,2048]{1,0:T(8,128)(2,1)}, u32[]{:S(2)}, u32[]{:S(2)}) collective-permute-start(bf16[256,2048]{1,0:T(8,128)(2,1)} %get-tuple-element.50), channel_id=1, source_target_pairs={{0,8},{4,12},{8,16},{12,20},{16,24},{20,28},{1,9},{5,13},{9,17},{1... | collective-permute-start | bytes 3145736 | tf_op jit(solution)/shard_map/ppermute | solution.py:138
  331.2 5.3 %collective-permute-done.10 = bf16[256,2048]{1,0:T(8,128)(2,1)} collective-permute-done((bf16[256,2048]{1,0:T(8,128)(2,1)}, bf16[256,2048]{1,0:T(8,128)(2,1)}, u32[]{:S(2)}, u32[]{:S(2)}) %collective-permute-start.10) | collective-permute-done | bytes 1048608 | tf_op jit(solution)/shard_map/ppermute | solution.py:138
  336.5 12.2 %collective-permute-done.13 = bf16[256,2048]{1,0:T(8,128)(2,1)} collective-permute-done((bf16[256,2048]{1,0:T(8,128)(2,1)}, bf16[256,2048]{1,0:T(8,128)(2,1)}, u32[]{:S(2)}, u32[]{:S(2)}) %collective-permute-start.13) | collective-permute-done | bytes 1048608 | tf_op jit(solution)/shard_map/ppermute | solution.py:139
  355.2 11.6 %collective-permute-done.6 = bf16[256,2048]{1,0:T(8,128)(2,1)} collective-permute-done((bf16[256,2048]{1,0:T(8,128)(2,1)}, bf16[256,2048]{1,0:T(8,128)(2,1)}, u32[]{:S(2)}, u32[]{:S(2)}) %collective-permute-start.6) | collective-permute-done | bytes 1048608 | tf_op jit(solution)/shard_map/ppermute | solution.py:139
  366.8 3.9 multiply_reduce_fusion.8
  373.4 11.3 %shard_map.195 = (f32[56,128]{1,0:T(8,128)S(1)}, f32[32,128]{1,0:T(8,128)S(1)}) custom-call(f32[56,128]{1,0:T(8,128)S(1)} %pad_bitcast_fusion.dp_ref, f32[8,128]{1,0:T(8,128)S(1)} %fusion.8.mp_ref), custom_call_target="tpu_custom_call" | custom-call | tf_op jit(solution)/shard_map/pallas_call | solution.py:89
  397.8 9.0 %shard_map.196 = (f32[8,128]{1,0:T(8,128)}, f32[16,128]{1,0:T(8,128)S(1)}) custom-call(f32[8,128]{1,0:T(8,128)S(1)} %fusion.7.dp_ref, f32[8,128]{1,0:T(8,128)S(1)} %broadcast_in_dim.2.mp_ref), custom_call_target="tpu_custom_call" | custom-call | tf_op jit(solution)/shard_map/pallas_call | solution.py:89
  (134 shorter events, 87.4 us)
Async XLA Ops:
  7.2 47.2 %copy-start = (bf16[768,2048]{1,0:T(8,128)(2,1)S(1)}, bf16[768,2048]{1,0:T(8,128)(2,1)}, u32[]{:S(2)}) copy-start(bf16[768,2048]{1,0:T(8,128)(2,1)} %param.13) | copy-start | bytes 9437188
  7.2 407.6 %reduce-scatter.2.cloned.1.call-start = ((), (), s32[]{:S(2)}) async-start(), calls=%async_computation.1 | async-start | bytes 3932160 | tf_op jit(solution)/shard_map/reduce_scatter | solution.py:201
  60.7 16.2 %collective-permute-start.14 = (bf16[1024,2048]{1,0:T(8,128)(2,1)}, bf16[1024,2048]{1,0:T(8,128)(2,1)}, u32[]{:S(2)}, u32[]{:S(2)}) collective-permute-start(bf16[1024,2048]{1,0:T(8,128)(2,1)} %multiply_convert_fusion.5), channel_id=1, source_target_pairs={{0,4},{4,0},{8,12},{12,8},{16,20},{20,16},{24,28},{28,24},{1,5},{5... | collective-permute-start | bytes 12582920 | tf_op jit(solution)/shard_map/ppermute | solution.py:175
  106.7 64.9 %collective-permute-start.7 = (bf16[1024,2048]{1,0:T(8,128)(2,1)}, bf16[1024,2048]{1,0:T(8,128)(2,1)}, u32[]{:S(2)}, u32[]{:S(2)}) collective-permute-start(bf16[1024,2048]{1,0:T(8,128)(2,1)} %multiply_convert_fusion.1), channel_id=1, source_target_pairs={{0,4},{4,0},{8,12},{12,8},{16,20},{20,16},{24,28},{28,24},{1,5},{5... | collective-permute-start | bytes 12582920 | tf_op jit(solution)/shard_map/ppermute | solution.py:175
  110.0 27.4 %collective-permute-start.15 = (bf16[256,2048]{1,0:T(8,128)(2,1)}, bf16[256,2048]{1,0:T(8,128)(2,1)}, u32[]{:S(2)}, u32[]{:S(2)}) collective-permute-start(bf16[256,2048]{1,0:T(8,128)(2,1)} %get-tuple-element.48), channel_id=1, source_target_pairs={{0,8},{4,12},{1,9},{5,13},{2,10},{6,14},{3,11},{7,15}} | collective-permute-start | bytes 3145736 | tf_op jit(solution)/shard_map/ppermute | solution.py:138
  118.1 61.9 %collective-permute-start = (bf16[1024,2048]{1,0:T(8,128)(2,1)}, bf16[1024,2048]{1,0:T(8,128)(2,1)}, u32[]{:S(2)}, u32[]{:S(2)}) collective-permute-start(bf16[1024,2048]{1,0:T(8,128)(2,1)} %multiply_convert_fusion.3), channel_id=1, source_target_pairs={{0,4},{4,0},{8,12},{12,8},{16,20},{20,16},{24,28},{28,24},{1,5},{5... | collective-permute-start | bytes 12582920 | tf_op jit(solution)/shard_map/ppermute | solution.py:175
  118.2 23.7 %collective-permute-start.18 = (bf16[256,2048]{1,0:T(8,128)(2,1)S(1)}, bf16[256,2048]{1,0:T(8,128)(2,1)}, u32[]{:S(2)}, u32[]{:S(2)}) collective-permute-start(bf16[256,2048]{1,0:T(8,128)(2,1)S(1)} %get-tuple-element.49), channel_id=1, source_target_pairs={{24,16},{28,20},{25,17},{29,21},{26,18},{30,22},{27,19},{31,23}} | collective-permute-start | bytes 3145736 | tf_op jit(solution)/shard_map/ppermute | solution.py:139
  140.0 26.6 %collective-permute-start.16 = (bf16[256,2048]{1,0:T(8,128)(2,1)}, bf16[256,2048]{1,0:T(8,128)(2,1)}, u32[]{:S(2)}, u32[]{:S(2)}) collective-permute-start(bf16[256,2048]{1,0:T(8,128)(2,1)} %bitcast_add_fusion.2), channel_id=1, source_target_pairs={{0,8},{4,12},{8,16},{12,20},{1,9},{5,13},{9,17},{13,21},{2,10},{6,... | collective-permute-start | bytes 3145736 | tf_op jit(solution)/shard_map/ppermute | solution.py:138
  170.3 25.6 %collective-permute-start.19 = (bf16[256,2048]{1,0:T(8,128)(2,1)}, bf16[256,2048]{1,0:T(8,128)(2,1)}, u32[]{:S(2)}, u32[]{:S(2)}) collective-permute-start(bf16[256,2048]{1,0:T(8,128)(2,1)} %get-tuple-element.47), channel_id=1, source_target_pairs={{16,8},{20,12},{24,16},{28,20},{17,9},{21,13},{25,17},{29,21},{18,... | collective-permute-start | bytes 3145736 | tf_op jit(solution)/shard_map/ppermute | solution.py:139
  178.4 28.6 %collective-permute-start.8 = (bf16[256,2048]{1,0:T(8,128)(2,1)}, bf16[256,2048]{1,0:T(8,128)(2,1)}, u32[]{:S(2)}, u32[]{:S(2)}) collective-permute-start(bf16[256,2048]{1,0:T(8,128)(2,1)} %get-tuple-element.52), channel_id=1, source_target_pairs={{0,8},{4,12},{1,9},{5,13},{2,10},{6,14},{3,11},{7,15}} | collective-permute-start | bytes 3145736 | tf_op jit(solution)/shard_map/ppermute | solution.py:138
  189.4 40.1 %collective-permute-start.1 = (bf16[256,2048]{1,0:T(8,128)(2,1)}, bf16[256,2048]{1,0:T(8,128)(2,1)}, u32[]{:S(2)}, u32[]{:S(2)}) collective-permute-start(bf16[256,2048]{1,0:T(8,128)(2,1)} %get-tuple-element.56), channel_id=1, source_target_pairs={{0,8},{4,12},{1,9},{5,13},{2,10},{6,14},{3,11},{7,15}} | collective-permute-start | bytes 3145736 | tf_op jit(solution)/shard_map/ppermute | solution.py:138
  190.7 38.8 %copy-start.5 = (bf16[1024,2048]{1,0:T(8,128)(2,1)S(1)}, bf16[1024,2048]{1,0:T(8,128)(2,1)}, u32[]{:S(2)}) copy-start(bf16[1024,2048]{1,0:T(8,128)(2,1)} %copy-done.4) | copy-start | bytes 12582916
  190.7 134.3 %collective-permute-start.17 = (bf16[256,2048]{1,0:T(8,128)(2,1)}, bf16[256,2048]{1,0:T(8,128)(2,1)S(1)}, u32[]{:S(2)}, u32[]{:S(2)}) collective-permute-start(bf16[256,2048]{1,0:T(8,128)(2,1)} %get-tuple-element.46), channel_id=1, source_target_pairs={{0,8},{4,12},{8,16},{12,20},{16,24},{20,28},{1,9},{5,13},{9,17},{1... | collective-permute-start | bytes 3145736 | tf_op jit(solution)/shard_map/ppermute | solution.py:138
  198.6 46.5 %collective-permute-start.11 = (bf16[256,2048]{1,0:T(8,128)(2,1)S(1)}, bf16[256,2048]{1,0:T(8,128)(2,1)S(1)}, u32[]{:S(2)}, u32[]{:S(2)}) collective-permute-start(bf16[256,2048]{1,0:T(8,128)(2,1)S(1)} %copy-done.17), channel_id=1, source_target_pairs={{24,16},{28,20},{25,17},{29,21},{26,18},{30,22},{27,19},{31,23}} | collective-permute-start | bytes 3145736 | tf_op jit(solution)/shard_map/ppermute | solution.py:139
  199.3 77.8 %collective-permute-start.4 = (bf16[256,2048]{1,0:T(8,128)(2,1)S(1)}, bf16[256,2048]{1,0:T(8,128)(2,1)S(1)}, u32[]{:S(2)}, u32[]{:S(2)}) collective-permute-start(bf16[256,2048]{1,0:T(8,128)(2,1)S(1)} %get-tuple-element.57), channel_id=1, source_target_pairs={{24,16},{28,20},{25,17},{29,21},{26,18},{30,22},{27,19},{31,23}} | collective-permute-start | bytes 3145736 | tf_op jit(solution)/shard_map/ppermute | solution.py:139
  207.0 89.9 %slice-start = ((s8[8388608]{0:T(1024)(128)(4,1)}), s8[4194304]{0:T(1024)(128)(4,1)S(1)}, s32[]{:S(2)}) async-start(s8[8388608]{0:T(1024)(128)(4,1)} %bitcast.144), calls=%async_computation.2 | async-start | bytes 8388608
  208.8 65.5 %collective-permute-start.9 = (bf16[256,2048]{1,0:T(8,128)(2,1)S(1)}, bf16[256,2048]{1,0:T(8,128)(2,1)S(1)}, u32[]{:S(2)}, u32[]{:S(2)}) collective-permute-start(bf16[256,2048]{1,0:T(8,128)(2,1)S(1)} %bitcast_add_fusion.6), channel_id=1, source_target_pairs={{0,8},{4,12},{8,16},{12,20},{1,9},{5,13},{9,17},{13,21},{2,10},{6,... | collective-permute-start | bytes 3145736 | tf_op jit(solution)/shard_map/ppermute | solution.py:138
  230.8 43.5 %copy-start.7 = (bf16[1024,2048]{1,0:T(8,128)(2,1)S(1)}, bf16[1024,2048]{1,0:T(8,128)(2,1)}, u32[]{:S(2)}) copy-start(bf16[1024,2048]{1,0:T(8,128)(2,1)} %copy-done.6) | copy-start | bytes 12582916
  230.8 66.1 %slice-start.1 = ((s8[8388608]{0:T(1024)(128)(4,1)}), s8[4194304]{0:T(1024)(128)(4,1)S(1)}, s32[]{:S(2)}) async-start(s8[8388608]{0:T(1024)(128)(4,1)} %bitcast.144), calls=%async_computation.3 | async-start | bytes 8388608
  230.8 63.3 %collective-permute-start.2 = (bf16[256,2048]{1,0:T(8,128)(2,1)S(1)}, bf16[256,2048]{1,0:T(8,128)(2,1)S(1)}, u32[]{:S(2)}, u32[]{:S(2)}) collective-permute-start(bf16[256,2048]{1,0:T(8,128)(2,1)S(1)} %bitcast_add_fusion.10), channel_id=1, source_target_pairs={{0,8},{4,12},{8,16},{12,20},{1,9},{5,13},{9,17},{13,21},{2,10},{6,... | collective-permute-start | bytes 3145736 | tf_op jit(solution)/shard_map/ppermute | solution.py:138
  245.0 83.4 %collective-permute-start.20 = (bf16[256,2048]{1,0:T(8,128)(2,1)}, bf16[256,2048]{1,0:T(8,128)(2,1)S(1)}, u32[]{:S(2)}, u32[]{:S(2)}) collective-permute-start(bf16[256,2048]{1,0:T(8,128)(2,1)} %bitcast_add_fusion.1), channel_id=1, source_target_pairs={{8,0},{12,4},{16,8},{20,12},{24,16},{28,20},{9,1},{13,5},{17,9},{2... | collective-permute-start | bytes 3145736 | tf_op jit(solution)/shard_map/ppermute | solution.py:139
  275.8 36.8 %collective-permute-start.12 = (bf16[256,2048]{1,0:T(8,128)(2,1)}, bf16[256,2048]{1,0:T(8,128)(2,1)}, u32[]{:S(2)}, u32[]{:S(2)}) collective-permute-start(bf16[256,2048]{1,0:T(8,128)(2,1)} %get-tuple-element.51), channel_id=1, source_target_pairs={{16,8},{20,12},{24,16},{28,20},{17,9},{21,13},{25,17},{29,21},{18,... | collective-permute-start | bytes 3145736 | tf_op jit(solution)/shard_map/ppermute | solution.py:139
  295.6 24.8 %collective-permute-start.5 = (bf16[256,2048]{1,0:T(8,128)(2,1)}, bf16[256,2048]{1,0:T(8,128)(2,1)}, u32[]{:S(2)}, u32[]{:S(2)}) collective-permute-start(bf16[256,2048]{1,0:T(8,128)(2,1)} %get-tuple-element.55), channel_id=1, source_target_pairs={{16,8},{20,12},{24,16},{28,20},{17,9},{21,13},{25,17},{29,21},{18,... | collective-permute-start | bytes 3145736 | tf_op jit(solution)/shard_map/ppermute | solution.py:139
  308.0 28.5 %collective-permute-start.10 = (bf16[256,2048]{1,0:T(8,128)(2,1)}, bf16[256,2048]{1,0:T(8,128)(2,1)}, u32[]{:S(2)}, u32[]{:S(2)}) collective-permute-start(bf16[256,2048]{1,0:T(8,128)(2,1)} %get-tuple-element.50), channel_id=1, source_target_pairs={{0,8},{4,12},{8,16},{12,20},{16,24},{20,28},{1,9},{5,13},{9,17},{1... | collective-permute-start | bytes 3145736 | tf_op jit(solution)/shard_map/ppermute | solution.py:138
  312.6 42.6 %collective-permute-start.3 = (bf16[256,2048]{1,0:T(8,128)(2,1)}, bf16[256,2048]{1,0:T(8,128)(2,1)S(1)}, u32[]{:S(2)}, u32[]{:S(2)}) collective-permute-start(bf16[256,2048]{1,0:T(8,128)(2,1)} %get-tuple-element.54), channel_id=1, source_target_pairs={{0,8},{4,12},{8,16},{12,20},{16,24},{20,28},{1,9},{5,13},{9,17},{1... | collective-permute-start | bytes 3145736 | tf_op jit(solution)/shard_map/ppermute | solution.py:138
  320.4 28.3 %collective-permute-start.13 = (bf16[256,2048]{1,0:T(8,128)(2,1)}, bf16[256,2048]{1,0:T(8,128)(2,1)}, u32[]{:S(2)}, u32[]{:S(2)}) collective-permute-start(bf16[256,2048]{1,0:T(8,128)(2,1)} %bitcast_add_fusion.5), channel_id=1, source_target_pairs={{8,0},{12,4},{16,8},{20,12},{24,16},{28,20},{9,1},{13,5},{17,9},{2... | collective-permute-start | bytes 3145736 | tf_op jit(solution)/shard_map/ppermute | solution.py:139
  325.0 41.8 %collective-permute-start.6 = (bf16[256,2048]{1,0:T(8,128)(2,1)}, bf16[256,2048]{1,0:T(8,128)(2,1)}, u32[]{:S(2)}, u32[]{:S(2)}) collective-permute-start(bf16[256,2048]{1,0:T(8,128)(2,1)} %bitcast_add_fusion.9), channel_id=1, source_target_pairs={{8,0},{12,4},{16,8},{20,12},{24,16},{28,20},{9,1},{13,5},{17,9},{2... | collective-permute-start | bytes 3145736 | tf_op jit(solution)/shard_map/ppermute | solution.py:139
  331.2 54.2 %copy-start.23 = (f32[256]{0:T(256)}, f32[256]{0:T(256)S(1)}, u32[]{:S(2)}) copy-start(f32[256]{0:T(256)S(1)} %get-tuple-element.41) | copy-start | bytes 3076
  352.2 32.5 %copy-start.26 = (f32[3]{0:T(128)S(1)}, f32[3]{0:T(128)}, u32[]{:S(2)}) copy-start(f32[3]{0:T(128)} %constant.159) | copy-start | bytes 40
  352.2 35.7 %copy-start.18 = (f32[2048]{0:T(1024)S(1)}, f32[2048]{0:T(1024)}, u32[]{:S(2)}) copy-start(f32[2048]{0:T(1024)} %param.18) | copy-start | bytes 24580
  352.3 35.7 %copy-start.19 = (f32[2048]{0:T(1024)S(1)}, f32[2048]{0:T(1024)}, u32[]{:S(2)}) copy-start(f32[2048]{0:T(1024)} %param.20) | copy-start | bytes 24580
  352.3 35.7 %copy-start.20 = (f32[2048]{0:T(1024)S(1)}, f32[2048]{0:T(1024)}, u32[]{:S(2)}) copy-start(f32[2048]{0:T(1024)} %param.22) | copy-start | bytes 24580
  (22 other events, 249.9 us)
Sparse Core Ops, SparseCore 0:
  308.2 45.0 reduce-scatter.1
